TPU v7x, 32 devices: a whole 2x2x4 slice. The times are simulated.
32 devices in a mesh: groups: 2 (over x), expert: 16 (over z, y, core).
Axes of the slice: x: 2, y: 2, z: 4, core: 2. Of those that a mesh axis runs over, the one named last changes fastest.
Arguments:
- tokens: bfloat16 [4096, 2048], P(('groups', 'expert')), parts along dimension 0, may hold values from -6 to 6
- cotangent: bfloat16 [4096, 2048], P(('groups', 'expert')), parts along dimension 0, may hold values from -6 to 6
- route_probs: bfloat16 [4096, 2], P(('groups', 'expert')), parts along dimension 0, may hold values from 0.099609375 to 1
- expert_ids: int32 [4096, 2], P(('groups', 'expert')), parts along dimension 0, may hold values from 0 to 7, all different within a row; in each aligned block of 128 rows (0 to 127, 128 to 255, ...) at most 64 rows name the same one
- w_gate: bfloat16 [32, 2048, 384], P(('groups', 'expert')), parts along dimension 0, may hold values from -0.125 to 0.125
- w_up: bfloat16 [32, 2048, 384], P(('groups', 'expert')), parts along dimension 0, may hold values from -0.125 to 0.125
- w_down: bfloat16 [32, 384, 2048], P(('groups', 'expert')), parts along dimension 0, may hold values from -0.21875 to 0.21875
Outputs:
- token_grad: bfloat16 [4096, 2048], P(('groups', 'expert')), parts along dimension 0
- prob_grad: bfloat16 [4096, 2], P(('groups', 'expert')), parts along dimension 0
- gate_wgrad: bfloat16 [32, 2048, 384], P(('groups', 'expert')), parts along dimension 0
- up_wgrad: bfloat16 [32, 2048, 384], P(('groups', 'expert')), parts along dimension 0
- down_wgrad: bfloat16 [32, 384, 2048], P(('groups', 'expert')), parts along dimension 0
There are 2 independent parts, one for each index of `groups`. A program takes and returns all parts, laid end to end along the dimension named above; each array names one. Nothing has to cross between parts.
Inputs may be any that keep to these rules, and one draw needn't show every extreme that they name: `expert_ids`: A token's 2 experts are distinct. Among the 128 tokens of one device (aligned blocks of rows), no expert is named by more than 64 tokens, a bound that some block reaches.
All inputs are finite; a program needn't handle non-finite values.
Results may differ from a plain program's by a relative error of at most 0.0095.
Values may be sent and summed in bfloat16 or wider, within the bound.
A program may use at most 128 MiB of HBM per device.

v0:
```python
import jax
import jax.numpy as jnp
from jax import lax
from jax.sharding import PartitionSpec as P


def half_backward(rows_x, rows_g, rows_p, gate_half, up_half, down_half):
    pre_gate = jnp.dot(rows_x, gate_half, preferred_element_type=jnp.float32)
    pre_up = jnp.dot(rows_x, up_half, preferred_element_type=jnp.float32)
    sigma = jax.nn.sigmoid(pre_gate)
    active = pre_gate * sigma
    hidden = (active * pre_up).astype(jnp.bfloat16)
    back_hidden = jnp.dot(rows_g, down_half.T, preferred_element_type=jnp.float32)
    gate_part = jnp.sum(back_hidden * hidden.astype(jnp.float32), axis=1).astype(jnp.bfloat16)
    weight_rows = rows_p.astype(jnp.float32)[:, None]
    scaled_hidden = weight_rows * back_hidden
    grad_pre = (scaled_hidden * pre_up * sigma * (1.0 + pre_gate * (1.0 - sigma))).astype(
        jnp.bfloat16
    )
    grad_up = (scaled_hidden * active).astype(jnp.bfloat16)
    scaled_cot = (weight_rows * rows_g.astype(jnp.float32)).astype(jnp.bfloat16)
    down_grad = jnp.dot(hidden.T, scaled_cot, preferred_element_type=jnp.float32).astype(
        jnp.bfloat16
    )
    gate_grad = jnp.dot(rows_x.T, grad_pre, preferred_element_type=jnp.float32).astype(jnp.bfloat16)
    up_grad = jnp.dot(rows_x.T, grad_up, preferred_element_type=jnp.float32).astype(jnp.bfloat16)
    input_part = (
        jnp.dot(grad_pre, gate_half.T, preferred_element_type=jnp.float32)
        + jnp.dot(grad_up, up_half.T, preferred_element_type=jnp.float32)
    ).astype(jnp.bfloat16)
    return (input_part, gate_part, gate_grad, up_grad, down_grad)


def local(tokens, cotangent, route_probs, expert_ids, w_gate, w_up, w_down):
    tok_count = tokens.shape[0]
    d_model = tokens.shape[1]
    per_token = expert_ids.shape[1]
    devices = lax.axis_size("expert")
    experts = devices // 2
    capacity = 2 * (tok_count * per_token // experts)
    pair_count = tok_count * per_token
    flat_ids = expert_ids.reshape(-1)
    onehot = (flat_ids[:, None] == jnp.arange(experts, dtype=jnp.int32)[None, :]).astype(jnp.int32)
    ranks = jnp.sum((jnp.cumsum(onehot, axis=0) - 1) * onehot, axis=1)
    place = flat_ids * capacity + ranks
    source = (
        jnp.full((experts * capacity,), pair_count, jnp.int32)
        .at[place]
        .set(jnp.arange(pair_count, dtype=jnp.int32))
    )
    tok_pad = jnp.concatenate([tokens, jnp.zeros((1, d_model), tokens.dtype)], axis=0)
    cot_pad = jnp.concatenate([cotangent, jnp.zeros((1, d_model), cotangent.dtype)], axis=0)
    prob_pad = jnp.concatenate(
        [route_probs.reshape(-1), jnp.zeros((1,), route_probs.dtype)], axis=0
    )
    send_x = tok_pad[source // per_token]
    send_g = cot_pad[source // per_token]
    send_p = prob_pad[source]
    got_x, got_g, got_p = (
        lax.all_to_all(
            jnp.repeat(send_x.reshape(experts, capacity, d_model), 2, axis=0),
            "expert",
            split_axis=0,
            concat_axis=0,
            tiled=True,
        ),
        lax.all_to_all(
            jnp.repeat(send_g.reshape(experts, capacity, d_model), 2, axis=0),
            "expert",
            split_axis=0,
            concat_axis=0,
            tiled=True,
        ),
        lax.all_to_all(
            jnp.repeat(send_p.reshape(experts, capacity), 2, axis=0),
            "expert",
            split_axis=0,
            concat_axis=0,
            tiled=True,
        ),
    )
    input_part, gate_part, gate_grad, up_grad, down_grad = half_backward(
        got_x.reshape(-1, d_model),
        got_g.reshape(-1, d_model),
        got_p.reshape(-1),
        w_gate[0],
        w_up[0],
        w_down[0],
    )
    part_rows = input_part.reshape(devices, capacity, d_model)
    part_gate = gate_part.reshape(devices, capacity)
    back_rows, back_gate = (
        lax.all_to_all(part_rows, "expert", split_axis=0, concat_axis=0, tiled=True),
        lax.all_to_all(part_gate, "expert", split_axis=0, concat_axis=0, tiled=True),
    )
    result_rows = (
        back_rows.reshape(experts, 2, capacity, d_model)
        .astype(jnp.float32)
        .sum(axis=1)
        .astype(jnp.bfloat16)
        .reshape(-1, d_model)
    )
    result_gate = (
        back_gate.reshape(experts, 2, capacity)
        .astype(jnp.float32)
        .sum(axis=1)
        .astype(jnp.bfloat16)
        .reshape(-1)
    )
    pair_rows = result_rows[place]
    token_grad = (
        pair_rows.reshape(tok_count, per_token, d_model)
        .astype(jnp.float32)
        .sum(axis=1)
        .astype(jnp.bfloat16)
    )
    prob_grad = result_gate[place].reshape(tok_count, per_token)
    return (token_grad, prob_grad, gate_grad[None], up_grad[None], down_grad[None])


def solution(mesh):
    in_specs = (
        P(("groups", "expert"), None),
        P(("groups", "expert"), None),
        P(("groups", "expert"), None),
        P(("groups", "expert"), None),
        P(("groups", "expert"), None, None),
        P(("groups", "expert"), None, None),
        P(("groups", "expert"), None, None),
    )
    out_specs = (
        P(("groups", "expert"), None),
        P(("groups", "expert"), None),
        P(("groups", "expert"), None, None),
        P(("groups", "expert"), None, None),
        P(("groups", "expert"), None, None),
    )
    return jax.shard_map(local, mesh=mesh, in_specs=in_specs, out_specs=out_specs, check_vma=False)
```

profile of v0, /device:TPU:15, one launch (start us, length us, event | category | flops | bytes accessed | tf_op | source)
XLA Modules:
  0.0 360.9 jit_solution(3307258865250101963)
XLA Ops:
  0.6 0.0 copy-start
  0.6 0.8 broadcast_multiply_fusion
  1.4 0.8 copy.25
  2.2 0.1 eq.29
  2.4 0.1 eq.25
  2.5 0.8 copy.23
  3.3 0.1 reshape.132
  3.5 0.1 copy.24
  3.6 0.1 mul.61
  3.7 0.6 reduce-window.6
  4.3 0.2 slice_reduce_fusion
  4.6 0.1 fusion.16
  4.7 1.4 scatter_custom_fusion
  6.1 3.5 gather_fusion
  9.7 0.1 reshape.134
  9.7 0.6 copy.27
  10.4 6.6 %all-to-all-start = ((bf16[16,1,64]{2,1,0:T(2,128)(2,1)}), bf16[16,1,64]{2,1,0:T(2,128)(2,1)S(1)}, u32[]{:S(2)}, u32[]{:S(2)}) async-start(bf16[16,1,64]{2,1,0:T(2,128)(2,1)} %copy.27), calls=%async_computation | async-start | bytes 16384 | tf_op jit(solution)/shard_map/all_to_all | solution.py:74
  16.9 1.1 concatenate.11
  18.0 3.3 gather_fusion.2
  21.4 4.1 %broadcast_in_dim.38 = bf16[8,2,64,2048]{3,2,1,0:T(8,128)(2,1)} broadcast(bf16[8,64,2048]{2,1,0:T(8,128)(2,1)} %bitcast.57), dimensions={0,2,3} | broadcast | bytes 6291456 | tf_op jit(solution)/shard_map/broadcast_in_dim | solution.py:61
  25.5 6.4 %all-to-all-start.2 = ((bf16[16,64,2048]{2,1,0:T(8,128)(2,1)}), bf16[16,64,2048]{2,1,0:T(8,128)(2,1)}, u32[]{:S(2)}, u32[]{:S(2)}) async-start(bf16[16,64,2048]{2,1,0:T(8,128)(2,1)} %bitcast.55), calls=%async_computation.2 | async-start | bytes 8388608 | tf_op jit(solution)/shard_map/all_to_all | solution.py:60
  31.9 3.3 gather_fusion.1
  35.2 89.1 %all-to-all-done.2 = bf16[16,64,2048]{2,1,0:T(8,128)(2,1)} async-done(((bf16[16,64,2048]{2,1,0:T(8,128)(2,1)}), bf16[16,64,2048]{2,1,0:T(8,128)(2,1)}, u32[]{:S(2)}, u32[]{:S(2)}) %all-to-all-start.2) | async-done | bytes 4194336 | tf_op jit(solution)/shard_map/all_to_all | solution.py:60
  124.4 4.1 %broadcast_in_dim.37 = bf16[8,2,64,2048]{3,2,1,0:T(8,128)(2,1)} broadcast(bf16[8,64,2048]{2,1,0:T(8,128)(2,1)} %bitcast.56), dimensions={0,2,3} | broadcast | bytes 6291456 | tf_op jit(solution)/shard_map/broadcast_in_dim | solution.py:68
  128.5 4.9 %all-to-all-start.1 = ((bf16[16,64,2048]{2,1,0:T(8,128)(2,1)}), bf16[16,64,2048]{2,1,0:T(8,128)(2,1)}, u32[]{:S(2)}, u32[]{:S(2)}) async-start(bf16[16,64,2048]{2,1,0:T(8,128)(2,1)} %bitcast.54), calls=%async_computation.1 | async-start | bytes 8388608 | tf_op jit(solution)/shard_map/all_to_all | solution.py:67
  133.4 0.1 reshape.148
  133.5 5.3 %fusion.8 = f32[1024,384]{0,1:T(8,128)} fusion(bf16[1024,2048]{1,0:T(8,128)(2,1)} %bitcast.11, bf16[1,2048,384]{2,1,0:T(8,128)(2,1)S(1)} %copy-done), kind=kOutput, calls=%fused_computation.19 | convolution fusion | flops 1610612736 | bytes 7340032 | tf_op jit(solution)/shard_map/dot_general | solution.py:8
  138.8 5.2 %fusion.11 = f32[1024,384]{0,1:T(8,128)} fusion(bf16[1024,2048]{1,0:T(8,128)(2,1)} %bitcast.11, bf16[1,2048,384]{2,1,0:T(8,128)(2,1)S(1)} %copy-done.1), kind=kOutput, calls=%fused_computation.22 | convolution fusion | flops 1610612736 | bytes 7340032 | tf_op jit(solution)/shard_map/dot_general | solution.py:9
  143.9 81.9 %all-to-all-done.1 = bf16[16,64,2048]{2,1,0:T(8,128)(2,1)} async-done(((bf16[16,64,2048]{2,1,0:T(8,128)(2,1)}), bf16[16,64,2048]{2,1,0:T(8,128)(2,1)}, u32[]{:S(2)}, u32[]{:S(2)}) %all-to-all-start.1) | async-done | bytes 4194336 | tf_op jit(solution)/shard_map/all_to_all | solution.py:67
  225.8 7.4 %multiply_reduce_fusion = (bf16[1024]{0:T(1024)(128)(2,1)S(1)}, bf16[1024,384]{0,1:T(8,128)(2,1)}, bf16[1024,384]{0,1:T(8,128)(2,1)}, bf16[1024,384]{0,1:T(8,128)(2,1)}) fusion(f32[1024,384]{0,1:T(8,128)} %fusion.11, f32[1024,384]{0,1:T(8,128)} %fusion.8, f32[1024]{0:T(1024)S(1)} %reshape.148, bf16[1024,2048]{1,0:T(8,128)(2,1)} %bitcast.7, ...), kind=kOutput, calls=%fused_computation.26 | convolution fusion | flops 1618082816 | bytes 11278336 | tf_op jit(solution)/shard_map/dot_general | solution.py:13
  233.3 0.7 convert_element_type.81
  233.9 4.9 %all-to-all-start.4 = ((bf16[16,1,64]{2,1,0:T(2,128)(2,1)}), bf16[16,1,64]{2,1,0:T(2,128)(2,1)S(1)}, u32[]{:S(2)}, u32[]{:S(2)}) async-start(bf16[16,1,64]{2,1,0:T(2,128)(2,1)} %convert_element_type.81), calls=%async_computation.4 | async-start | bytes 16384 | tf_op jit(solution)/shard_map/all_to_all | solution.py:94
  238.9 3.6 fusion.6
  242.5 4.4 %add_convert_fusion = bf16[1024,2048]{1,0:T(8,128)(2,1)} fusion(f32[1024,2048]{1,0:T(8,128)S(1)} %fusion.6, bf16[1024,384]{0,1:T(8,128)(2,1)S(1)} %copy-done.2, bf16[1,2048,384]{2,1,0:T(8,128)(2,1)S(1)} %copy-done.1), kind=kOutput, calls=%fused_computation.7 | convolution fusion | flops 1614807040 | bytes 14942208 | tf_op jit(solution)/shard_map/dot_general | solution.py:29
  246.9 0.0 all-to-all-done.4
  246.9 6.1 %all-to-all-start.3 = ((bf16[16,64,2048]{2,1,0:T(8,128)(2,1)}), bf16[16,64,2048]{2,1,0:T(8,128)(2,1)}, u32[]{:S(2)}, u32[]{:S(2)}) async-start(bf16[16,64,2048]{2,1,0:T(8,128)(2,1)} %bitcast.53), calls=%async_computation.3 | async-start | bytes 8388608 | tf_op jit(solution)/shard_map/all_to_all | solution.py:93
  253.1 5.8 %fusion.4 = bf16[1,2048,384]{2,1,0:T(8,128)(2,1)} fusion(bf16[1024,2048]{1,0:T(8,128)(2,1)} %bitcast.11, bf16[1024,384]{0,1:T(8,128)(2,1)S(1)} %copy-done.4), kind=kOutput, calls=%fused_computation.15 | convolution fusion | flops 1611399168 | bytes 6553600 | tf_op jit(solution)/shard_map/dot_general | solution.py:25
  258.9 5.8 %fusion.5 = bf16[1,2048,384]{2,1,0:T(8,128)(2,1)} fusion(bf16[1024,2048]{1,0:T(8,128)(2,1)} %bitcast.11, bf16[1024,384]{0,1:T(8,128)(2,1)S(1)} %copy-done.3), kind=kOutput, calls=%fused_computation.16 | convolution fusion | flops 1611399168 | bytes 6553600 | tf_op jit(solution)/shard_map/dot_general | solution.py:26
  264.7 5.2 %fusion.3 = bf16[1,384,2048]{2,1,0:T(8,128)(2,1)} fusion(bf16[1024,384]{0,1:T(8,128)(2,1)S(1)} %copy-done.6, bf16[1024,2048]{1,0:T(8,128)(2,1)} %bitcast.7, f32[1024]{0:T(1024)S(1)} %reshape.148), kind=kOutput, calls=%fused_computation.14 | convolution fusion | flops 1617690624 | bytes 6557696 | tf_op jit(solution)/shard_map/dot_general | solution.py:22
  269.9 0.1 reshape.146
  270.0 1.9 gather_fusion.4
  272.0 0.2 reshape.147
  272.1 0.6 copy.29
  272.7 72.8 %all-to-all-done.3 = bf16[16,64,2048]{2,1,0:T(8,128)(2,1)} async-done(((bf16[16,64,2048]{2,1,0:T(8,128)(2,1)}), bf16[16,64,2048]{2,1,0:T(8,128)(2,1)}, u32[]{:S(2)}, u32[]{:S(2)}) %all-to-all-start.3) | async-done | bytes 4194336 | tf_op jit(solution)/shard_map/all_to_all | solution.py:93
  345.5 5.1 %bitcast_reduce_fusion = bf16[8,64,2048]{2,1,0:T(8,128)(2,1)} fusion(bf16[16,64,2048]{2,1,0:T(8,128)(2,1)} %all-to-all-done.3), kind=kLoop, calls=%fused_computation.9 | loop fusion | flops 1048576 | bytes 6291456 | tf_op jit(solution)/shard_map/reduce_sum | solution.py:99
  350.6 4.2 %gather_fusion.3 = bf16[256,2048]{1,0:T(8,128)(2,1)S(1)} fusion(bf16[512,2048]{1,0:T(8,128)(2,1)} %bitcast.52, s32[1024]{0:T(1024)S(1)} %pad_clamp_fusion), kind=kCustom, calls=%fused_computation.3 | custom fusion | bytes 2098176 | tf_op jit(solution)/shard_map/gather | solution.py:110
  354.9 1.5 reshape.144
  356.4 4.6 %reduce_sum.59 = bf16[128,2048]{1,0:T(8,128)(2,1)} reduce(bf16[128,2,2048]{2,1,0:T(2,128)(2,1)} %reshape.144, bf16[]{:T(256)} %constant.41.clone.1), dimensions={1}, to_apply=%region_5.6 | reduce | flops 262144 | bytes 1572866 | tf_op jit(solution)/shard_map/reduce_sum | solution.py:114
  (28 shorter events, 0.2 us)
Async XLA Ops:
  0.6 132.8 %copy-start = (bf16[1,2048,384]{2,1,0:T(8,128)(2,1)S(1)}, bf16[1,2048,384]{2,1,0:T(8,128)(2,1)}, u32[]{:S(2)}) copy-start(bf16[1,2048,384]{2,1,0:T(8,128)(2,1)} %param.11) | copy-start | bytes 4718596
  10.4 11.0 %all-to-all-start = ((bf16[16,1,64]{2,1,0:T(2,128)(2,1)}), bf16[16,1,64]{2,1,0:T(2,128)(2,1)S(1)}, u32[]{:S(2)}, u32[]{:S(2)}) async-start(bf16[16,1,64]{2,1,0:T(2,128)(2,1)} %copy.27), calls=%async_computation | async-start | bytes 16384 | tf_op jit(solution)/shard_map/all_to_all | solution.py:74
  25.5 6.4 %copy-start.5 = (bf16[128,2048]{1,0:T(8,128)(2,1)S(1)}, bf16[128,2048]{1,0:T(8,128)(2,1)}, u32[]{:S(2)}) copy-start(bf16[128,2048]{1,0:T(8,128)(2,1)} %param.8) | copy-start | bytes 1572868
  25.5 98.9 %all-to-all-start.2 = ((bf16[16,64,2048]{2,1,0:T(8,128)(2,1)}), bf16[16,64,2048]{2,1,0:T(8,128)(2,1)}, u32[]{:S(2)}, u32[]{:S(2)}) async-start(bf16[16,64,2048]{2,1,0:T(8,128)(2,1)} %bitcast.55), calls=%async_computation.2 | async-start | bytes 8388608 | tf_op jit(solution)/shard_map/all_to_all | solution.py:60
  128.5 97.3 %all-to-all-start.1 = ((bf16[16,64,2048]{2,1,0:T(8,128)(2,1)}), bf16[16,64,2048]{2,1,0:T(8,128)(2,1)}, u32[]{:S(2)}, u32[]{:S(2)}) async-start(bf16[16,64,2048]{2,1,0:T(8,128)(2,1)} %bitcast.54), calls=%async_computation.1 | async-start | bytes 8388608 | tf_op jit(solution)/shard_map/all_to_all | solution.py:67
  133.5 5.3 %copy-start.1 = (bf16[1,2048,384]{2,1,0:T(8,128)(2,1)S(1)}, bf16[1,2048,384]{2,1,0:T(8,128)(2,1)}, u32[]{:S(2)}) copy-start(bf16[1,2048,384]{2,1,0:T(8,128)(2,1)} %param.12) | copy-start | bytes 4718596
  233.9 12.9 %all-to-all-start.4 = ((bf16[16,1,64]{2,1,0:T(2,128)(2,1)}), bf16[16,1,64]{2,1,0:T(2,128)(2,1)S(1)}, u32[]{:S(2)}, u32[]{:S(2)}) async-start(bf16[16,1,64]{2,1,0:T(2,128)(2,1)} %convert_element_type.81), calls=%async_computation.4 | async-start | bytes 16384 | tf_op jit(solution)/shard_map/all_to_all | solution.py:94
  238.8 3.6 copy-start.2
  246.9 6.2 %copy-start.4 = (bf16[1024,384]{0,1:T(8,128)(2,1)S(1)}, bf16[1024,384]{0,1:T(8,128)(2,1)}, u32[]{:S(2)}) copy-start(bf16[1024,384]{0,1:T(8,128)(2,1)} %get-tuple-element.22) | copy-start | bytes 2359300
  246.9 98.6 %all-to-all-start.3 = ((bf16[16,64,2048]{2,1,0:T(8,128)(2,1)}), bf16[16,64,2048]{2,1,0:T(8,128)(2,1)}, u32[]{:S(2)}, u32[]{:S(2)}) async-start(bf16[16,64,2048]{2,1,0:T(8,128)(2,1)} %bitcast.53), calls=%async_computation.3 | async-start | bytes 8388608 | tf_op jit(solution)/shard_map/all_to_all | solution.py:93
  253.1 5.8 %copy-start.3 = (bf16[1024,384]{0,1:T(8,128)(2,1)S(1)}, bf16[1024,384]{0,1:T(8,128)(2,1)}, u32[]{:S(2)}) copy-start(bf16[1024,384]{0,1:T(8,128)(2,1)} %get-tuple-element.23) | copy-start | bytes 2359300
  258.9 5.8 %copy-start.6 = (bf16[1024,384]{0,1:T(8,128)(2,1)S(1)}, bf16[1024,384]{0,1:T(8,128)(2,1)}, u32[]{:S(2)}) copy-start(bf16[1024,384]{0,1:T(8,128)(2,1)} %get-tuple-element.21) | copy-start | bytes 2359300
where the time goes:
time: 362 us; the launch traced here: 361 us
  waiting for transfers between devices  244 us (67%)
  matrix products  42.7 us (12%)
  local copies, waits for them, and re-layouts  33.4 us (9%)
  starting transfers between devices  28.9 us (8%)
  other arithmetic  11.3 us (3%)
    all_to_all x1, waiting for transfers between devices, local(): lax.all_to_all(jnp.repeat(send_x.reshape(experts, capacity, d_model), 2,...  89.1 us
    all_to_all x1, waiting for transfers between devices, local(): lax.all_to_all(jnp.repeat(send_g.reshape(experts, capacity, d_model), 2,...  81.9 us
    all_to_all x1, waiting for transfers between devices, local(): lax.all_to_all(part_rows, 'expert', split_axis=0, concat_axis=0, tiled=True)  72.8 us
    dot_general x1, matrix products, half_backward(): jnp.dot(rows_g, down_half.T, preferred_element_type=jnp.float32)  7.43 us
  transfers between devices with their start and end apart: 5, of which 3 were waited for; matrix products, arithmetic and copies ran while one was open for 13% of the time, Pallas kernels for 0%

commit v1 on v0

--- a/solution.py
+++ b/solution.py
@@ -1,6 +1,8 @@
 import jax
 import jax.numpy as jnp
 from jax import lax
+from jax.experimental import pallas as pl
+from jax.experimental.pallas import tpu as pltpu
 from jax.sharding import PartitionSpec as P
 
 
@@ -118,6 +120,442 @@
     return (token_grad, prob_grad, gate_grad[None], up_grad[None], down_grad[None])
 
 
+NZ, NY, NC = 4, 2, 2
+NS = NZ * NY * NC
+COLS = 512
+LIMIT = 56 * 2**20
+
+
+def place_of(index):
+    return index // (NY * NC), (index // NC) % NY, index % NC
+
+
+def index_of(z, y, c):
+    return z * (NY * NC) + y * NC + c
+
+
+def enter(me):
+    barrier = pltpu.get_barrier_semaphore()
+
+    def greet(i, carry):
+        pl.semaphore_signal(
+            barrier, inc=1, device_id={"expert": (me + i) % NS}, device_id_type=pl.DeviceIdType.MESH
+        )
+        return carry
+
+    lax.fori_loop(1, NS, greet, 0)
+    pl.semaphore_wait(barrier, NS - 1)
+
+
+def remote(src, dst, send, recv, target):
+    return pltpu.make_async_remote_copy(
+        src_ref=src,
+        dst_ref=dst,
+        send_sem=send,
+        recv_sem=recv,
+        device_id={"expert": target},
+        device_id_type=pl.DeviceIdType.MESH,
+    )
+
+
+def onehot_rows(metas, source, own, other, cap):
+    slot = lax.broadcasted_iota(jnp.int32, (cap, metas.shape[2]), 0).astype(jnp.float32)
+    mine = metas[source, pl.ds(own, 1), :]
+    theirs = metas[source, pl.ds(other, 1), :]
+    return jnp.concatenate([slot == mine, slot == theirs], axis=0).astype(jnp.bfloat16)
+
+
+def dispatch_kernel(
+    xg_ref, meta_ref, slots, metas, zbuf, ysend, loc_sem, meta_send, meta_recv,
+    up_send, dn_send, z_recv, y_send, y_recv, c_send, c_recv,
+):
+    me = lax.axis_index("expert")
+    z, y, c = place_of(me)
+    own, other = z * NY + y, z * NY + (1 - y)
+    cap = slots.shape[2]
+    width = slots.shape[3]
+    local_copy = pltpu.make_async_copy(xg_ref, zbuf.at[z], loc_sem)
+    local_copy.start()
+    metas[me] = meta_ref[...]
+    enter(me)
+
+    def meta_copy(source, target):
+        return remote(metas.at[source], metas.at[source], meta_send.at[target], meta_recv.at[source], target)
+
+    def give_meta(i, carry):
+        meta_copy(me, (me + i) % NS).start()
+        return carry
+
+    def take_meta(i, carry):
+        source = (me + i) % NS
+        meta_copy(source, source).wait_recv()
+        return carry
+
+    def done_meta(i, carry):
+        meta_copy(me, (me + i) % NS).wait_send()
+        return carry
+
+    local_copy.wait()
+
+    def up_copy(zz, a):
+        return remote(
+            zbuf.at[zz, a], zbuf.at[zz, a], up_send.at[zz, a], z_recv.at[zz, a], index_of(z + 1, y, c)
+        )
+
+    def dn_copy(zz, a):
+        return remote(
+            zbuf.at[zz, a], zbuf.at[zz, a], dn_send.at[zz, a], z_recv.at[zz, a], index_of(z - 1, y, c)
+        )
+
+    def y_copy(zz, a):
+        return remote(
+            ysend.at[a, zz],
+            slots.at[a, index_of(zz, y, c)],
+            y_send.at[a, zz],
+            y_recv.at[a, zz],
+            index_of(z, 1 - y, c),
+        )
+
+    def c_copy(source, a):
+        return remote(
+            slots.at[a, source],
+            slots.at[a, source],
+            c_send.at[a, source],
+            c_recv.at[a, source],
+            index_of(z, y, 1 - c),
+        )
+
+    def forward(zz, a, d):
+        if d > 0:
+            pltpu.make_async_copy(zbuf.at[zz, a], zbuf.at[zz, a], z_recv.at[zz, a]).wait()
+
+        @pl.when((zz <= z) & (z < NZ - 1))
+        def _():
+            up_copy(zz, a).start()
+
+        @pl.when((zz >= z) & (z > 0))
+        def _():
+            dn_copy(zz, a).start()
+
+    def pick(zz, a):
+        source = index_of(zz, y, c)
+        hot = onehot_rows(metas, source, own, other, cap)
+
+        @pl.loop(0, width // COLS)
+        def _(j):
+            cols = pl.ds(pl.multiple_of(j * COLS, COLS), COLS)
+            rows = jnp.dot(hot, zbuf[zz, a, :, cols], preferred_element_type=jnp.float32)
+            rows = rows.astype(jnp.bfloat16)
+            slots[a, source, :, cols] = rows[:cap]
+            ysend[a, zz, :, cols] = rows[cap:]
+
+        y_copy(zz, a).start()
+        c_copy(source, a).start()
+
+    def relay(zz, a):
+        source = index_of(zz, 1 - y, c)
+        pltpu.make_async_copy(slots.at[a, source], slots.at[a, source], y_recv.at[a, zz]).wait()
+        c_copy(source, a).start()
+
+    def each(d, fn):
+        if d == 0:
+            fn(z)
+        else:
+            pl.when(z >= d)(lambda: fn(z - d))
+            pl.when(z + d < NZ)(lambda: fn(z + d))
+
+    for a in range(2):
+        forward(z, a, 0)
+    lax.fori_loop(1, NS, give_meta, 0)
+    lax.fori_loop(1, NS, take_meta, 0)
+    for d in range(NZ):
+        for a in range(2):
+
+            def step(zz, a=a, d=d):
+                if d > 0:
+                    forward(zz, a, d)
+                pick(zz, a)
+
+            each(d, step)
+            if d > 0:
+                each(d - 1, lambda zz, a=a: relay(zz, a))
+    for a in range(2):
+        each(NZ - 1, lambda zz, a=a: relay(zz, a))
+
+    def finish(zz, carry):
+        for a in range(2):
+
+            @pl.when((zz <= z) & (z < NZ - 1))
+            def _():
+                up_copy(zz, a).wait_send()
+
+            @pl.when((zz >= z) & (z > 0))
+            def _():
+                dn_copy(zz, a).wait_send()
+
+            y_copy(zz, a).wait_send()
+            for yy in range(NY):
+                c_copy(index_of(zz, yy, c), a).wait_send()
+                c_copy(index_of(zz, yy, 1 - c), a).wait_recv()
+        return carry
+
+    lax.fori_loop(0, NZ, finish, 0)
+    lax.fori_loop(1, NS, done_meta, 0)
+
+
+def return_kernel(
+    part_ref, gate_ref, metas, token_ref, gates, half, pairs, dense, came,
+    h_send, h_recv, q_send, q_recv, y_send, y_recv, r_send, r_recv,
+):
+    me = lax.axis_index("expert")
+    z, y, c = place_of(me)
+    own, other = z * NY + y, z * NY + (1 - y)
+    cap = part_ref.shape[1]
+    width = part_ref.shape[2]
+    gates[me] = gate_ref[me]
+    enter(me)
+
+    def h_copy(zz, yy):
+        return remote(
+            part_ref.at[index_of(zz, yy, 1 - c)],
+            half.at[zz, yy],
+            h_send.at[zz, yy],
+            h_recv.at[zz, yy],
+            index_of(z, y, 1 - c),
+        )
+
+    def q_copy(target):
+        return remote(gate_ref.at[target], gates.at[me], q_send.at[target], q_recv.at[me], target)
+
+    def y_copy(zz):
+        return remote(
+            pairs.at[zz, 2],
+            pairs.at[zz, 1],
+            y_send.at[zz],
+            y_recv.at[zz],
+            index_of(z, 1 - y, c),
+        )
+
+    def r_copy(zz, way):
+        return remote(
+            dense.at[zz],
+            came.at[zz, way],
+            r_send.at[zz],
+            r_recv.at[zz, way],
+            index_of(z - 1 if way == 0 else z + 1, y, c),
+        )
+
+    def each(d, fn):
+        if d == 0:
+            fn(z)
+        else:
+            pl.when(z >= d)(lambda: fn(z - d))
+            pl.when(z + d < NZ)(lambda: fn(z + d))
+
+    def start_halves(zz):
+        for yy in range(NY):
+            h_copy(zz, yy).start()
+
+    for d in range(NZ - 1, -1, -1):
+        each(d, start_halves)
+
+    def give_gate(i, carry):
+        q_copy((me + i) % NS).start()
+        return carry
+
+    lax.fori_loop(1, NS, give_gate, 0)
+
+    def add_half(zz, yy, to):
+        source = index_of(zz, yy, c)
+        h_copy(zz, yy).wait_recv()
+
+        @pl.loop(0, width // COLS)
+        def _(j):
+            cols = pl.ds(pl.multiple_of(j * COLS, COLS), COLS)
+            pairs[zz, to, :, cols] = (
+                part_ref[source, :, cols].astype(jnp.float32) + half[zz, yy, :, cols].astype(jnp.float32)
+            ).astype(jnp.bfloat16)
+
+    def sum_halves(zz):
+        add_half(zz, 1 - y, 2)
+        y_copy(zz).start()
+        add_half(zz, y, 0)
+
+    def arrival(zz, way):
+        pltpu.make_async_copy(came.at[zz, way], came.at[zz, way], r_recv.at[zz, way]).wait()
+
+    def spread(zz, ways, out):
+        hot = onehot_rows(metas, index_of(zz, y, c), own, other, cap)
+        tokens = hot.shape[1]
+
+        @pl.loop(0, width // COLS)
+        def _(j):
+            cols = pl.ds(pl.multiple_of(j * COLS, COLS), COLS)
+            rows = jnp.concatenate([pairs[zz, 0, :, cols], pairs[zz, 1, :, cols]], axis=0)
+            total = lax.dot_general(
+                hot, rows, (((0,), (0,)), ((), ())), preferred_element_type=jnp.float32
+            )
+            out[:, cols] = total.astype(jnp.bfloat16)
+
+        def add(way):
+            arrival(zz, way)
+
+            @pl.loop(0, width // COLS)
+            def _(j):
+                cols = pl.ds(pl.multiple_of(j * COLS, COLS), COLS)
+                out[:, cols] = (
+                    out[:, cols].astype(jnp.float32) + came[zz, way, :, cols].astype(jnp.float32)
+                ).astype(jnp.bfloat16)
+
+        for way in ways:
+            if way == 0:
+                pl.when(z < NZ - 1)(lambda: add(0))
+            else:
+                pl.when(z > 0)(lambda: add(1))
+
+    for d in range(NZ - 1, -1, -1):
+        each(d, sum_halves)
+    for d in range(NZ - 1, 0, -1):
+
+        @pl.when(z >= d)
+        def _(d=d):
+            zz = z - d
+            y_copy(zz).wait_recv()
+            spread(zz, (0,), dense.at[zz])
+            r_copy(zz, 0).start()
+
+        @pl.when(z + d < NZ)
+        def _(d=d):
+            zz = z + d
+            y_copy(zz).wait_recv()
+            spread(zz, (1,), dense.at[zz])
+            r_copy(zz, 1).start()
+
+    y_copy(z).wait_recv()
+    spread(z, (0, 1), token_ref)
+
+    def finish(zz, carry):
+        for yy in range(NY):
+            h_copy(zz, yy).wait_send()
+        y_copy(zz).wait_send()
+
+        @pl.when(zz < z)
+        def _():
+            r_copy(zz, 0).wait_send()
+
+        @pl.when(zz > z)
+        def _():
+            r_copy(zz, 1).wait_send()
+
+        return carry
+
+    lax.fori_loop(0, NZ, finish, 0)
+
+    def done_gate(i, carry):
+        q_copy((me + i) % NS).wait_send()
+        source = (me + i) % NS
+        pltpu.make_async_copy(gates.at[source], gates.at[source], q_recv.at[source]).wait()
+        return carry
+
+    lax.fori_loop(1, NS, done_gate, 0)
+
+
+def route_tables(route_probs, expert_ids, experts):
+    tok_count = expert_ids.shape[0]
+    names = jnp.arange(experts, dtype=jnp.int32)
+    hit = expert_ids.T[:, None, :] == names[None, :, None]
+    routed = jnp.any(hit, axis=0)
+    order = jnp.arange(tok_count, dtype=jnp.int32)
+    before = (order[:, None] < order[None, :]).astype(jnp.bfloat16)
+    rank = jnp.dot(routed.astype(jnp.bfloat16), before, preferred_element_type=jnp.float32)
+    slot = jnp.where(routed, rank, -1.0)
+    prob = jnp.sum(jnp.where(hit, route_probs.T.astype(jnp.float32)[:, None, :], 0.0), axis=0)
+    return hit, jnp.concatenate([slot, prob], axis=0)
+
+
+def local_chips(tokens, cotangent, route_probs, expert_ids, w_gate, w_up, w_down):
+    tok_count, d_model = tokens.shape
+    per_token = expert_ids.shape[1]
+    experts = NS // 2
+    cap = 2 * (tok_count * per_token // experts)
+    hit, meta = route_tables(route_probs, expert_ids, experts)
+    vmem = pl.BlockSpec(memory_space=pltpu.VMEM)
+    hbm = pl.BlockSpec(memory_space=pl.ANY)
+    dma = pltpu.SemaphoreType.DMA
+    slots, metas = pl.pallas_call(
+        dispatch_kernel,
+        out_shape=(
+            jax.ShapeDtypeStruct((2, NS, cap, d_model), jnp.bfloat16),
+            jax.ShapeDtypeStruct((NS,) + meta.shape, jnp.float32),
+        ),
+        in_specs=[hbm, vmem],
+        out_specs=(vmem, vmem),
+        scratch_shapes=[
+            pltpu.VMEM((NZ, 2, tok_count, d_model), jnp.bfloat16),
+            pltpu.VMEM((2, NZ, cap, d_model), jnp.bfloat16),
+            dma(()),
+            dma((NS,)),
+            dma((NS,)),
+            dma((NZ, 2)),
+            dma((NZ, 2)),
+            dma((NZ, 2)),
+            dma((2, NZ)),
+            dma((2, NZ)),
+            dma((2, NS)),
+            dma((2, NS)),
+        ],
+        compiler_params=pltpu.CompilerParams(
+            collective_id=0, has_side_effects=True, vmem_limit_bytes=LIMIT
+        ),
+    )(jnp.stack([tokens, cotangent]), meta)
+    expert = lax.axis_index("expert") // 2
+    my_slot = lax.dynamic_index_in_dim(metas, expert, 1, keepdims=False)
+    my_prob = lax.dynamic_index_in_dim(metas, expert + experts, 1, keepdims=False)
+    number = jnp.arange(cap, dtype=jnp.int32).astype(jnp.float32)
+    hot = my_slot[:, None, :] == number[None, :, None]
+    rows_p = jnp.sum(jnp.where(hot, my_prob[:, None, :], 0.0), axis=2).reshape(-1)
+    input_part, gate_part, gate_grad, up_grad, down_grad = half_backward(
+        slots[0].reshape(-1, d_model),
+        slots[1].reshape(-1, d_model),
+        rows_p,
+        w_gate[0],
+        w_up[0],
+        w_down[0],
+    )
+    gate_slot = gate_part.reshape(NS, cap).astype(jnp.float32)
+    gate_tok = jnp.sum(jnp.where(hot, gate_slot[:, :, None], 0.0), axis=1)
+    gate_tok = jnp.broadcast_to(gate_tok[:, None, :], (NS, 8, tok_count))
+    token_grad, gates = pl.pallas_call(
+        return_kernel,
+        out_shape=(
+            jax.ShapeDtypeStruct((tok_count, d_model), jnp.bfloat16),
+            jax.ShapeDtypeStruct((NS, 8, tok_count), jnp.float32),
+        ),
+        in_specs=[vmem, vmem, vmem],
+        out_specs=(vmem, vmem),
+        scratch_shapes=[
+            pltpu.VMEM((NZ, NY, cap, d_model), jnp.bfloat16),
+            pltpu.VMEM((NZ, 3, cap, d_model), jnp.bfloat16),
+            pltpu.VMEM((NZ, tok_count, d_model), jnp.bfloat16),
+            pltpu.VMEM((NZ, 2, tok_count, d_model), jnp.bfloat16),
+            dma((NZ, NY)),
+            dma((NZ, NY)),
+            dma((NS,)),
+            dma((NS,)),
+            dma((NZ,)),
+            dma((NZ,)),
+            dma((NZ,)),
+            dma((NZ, 2)),
+        ],
+        compiler_params=pltpu.CompilerParams(
+            collective_id=1, has_side_effects=True, vmem_limit_bytes=LIMIT
+        ),
+    )(input_part.reshape(NS, cap, d_model), gate_tok, metas)
+    both = gates[:, 0, :].reshape(experts, 2, tok_count).sum(axis=1)
+    prob_grad = jnp.sum(jnp.where(hit, both[None], 0.0), axis=1).T.astype(jnp.bfloat16)
+    return (token_grad, prob_grad, gate_grad[None], up_grad[None], down_grad[None])
+
+
 def solution(mesh):
     in_specs = (
         P(("groups", "expert"), None),
@@ -135,4 +573,5 @@
         P(("groups", "expert"), None, None),
         P(("groups", "expert"), None, None),
     )
-    return jax.shard_map(local, mesh=mesh, in_specs=in_specs, out_specs=out_specs, check_vma=False)
+    body = local_chips if mesh.shape["expert"] == NS else local
+    return jax.shard_map(body, mesh=mesh, in_specs=in_specs, out_specs=out_specs, check_vma=False)

time: 362 us -> 194 us (0.54)
  the two profiles are of different devices: /device:TPU:15 before, /device:TPU:0 now
where the time goes in v1:
time: 194 us; the launch traced here: 193 us
  Pallas kernels  148 us (76%)
  matrix products  27.1 us (14%)
  local copies, waits for them, and re-layouts  10.5 us (5%)
  other arithmetic  6.94 us (4%)
    pallas_call x1, Pallas kernels, local_chips(): pl.pallas_call(dispatch_kernel, out_shape=(jax.ShapeDtypeStruct((2, NS, c...  96.2 us
    pallas_call x1, Pallas kernels, local_chips(): pl.pallas_call(return_kernel, out_shape=(jax.ShapeDtypeStruct((tok_count,...  51.8 us
    dot_general x1, matrix products, half_backward(): jnp.dot(hidden.T, scaled_cot, preferred_element_type=jnp.float32)  5.62 us
    dot_general x1, matrix products, half_backward(): jnp.dot(grad_up, up_half.T, preferred_element_type=jnp.float32)  4.38 us
    slice x1, local copies, waits for them, and re-layouts, local_chips(): slots[1].reshape(-1, d_model)  4.29 us

profile of v1, /device:TPU:0, one launch (start us, length us, event | category | flops | bytes accessed | tf_op | source)
XLA Modules:
  0.0 193.3 jit_solution(17419011307219012129)
XLA Ops:
  0.6 0.0 copy-start
  0.7 0.8 fusion.18
  1.5 0.1 convolution_select_fusion
  1.6 0.7 convert_bitcast_fusion
  2.3 0.7 select_reduce_fusion.1
  3.0 0.6 pad_maximum_fusion.1.meta_ref
  3.6 2.3 %pad_maximum_fusion.xg_ref = bf16[2,128,2048]{2,1,0:T(8,128)(2,1)} fusion(bf16[1,128,2048]{2,1,0:T(8,128)(2,1)} %bitcast.53, bf16[1,128,2048]{2,1,0:T(8,128)(2,1)} %bitcast.54), kind=kLoop, calls=%fused_computation.26 | loop fusion | flops 524288 | bytes 2097152 | tf_op jit(solution)/shard_map/stack | solution.py:510
  5.8 96.2 %shard_map.110 = (bf16[2,16,64,2048]{3,2,1,0:T(8,128)(2,1)}, f32[16,16,128]{2,1,0:T(8,128)}) custom-call(bf16[2,128,2048]{2,1,0:T(8,128)(2,1)} %pad_maximum_fusion.xg_ref, f32[16,128]{1,0:T(8,128)} %pad_maximum_fusion.1.meta_ref), custom_call_target="tpu_custom_call" | custom-call | tf_op jit(solution)/shard_map/pallas_call | solution.py:485
  102.0 0.9 constant_dynamic-slice_fusion
  102.9 0.0 copy-start.4
  102.9 4.3 %fusion.19 = (bf16[1,16,64,2048]{3,2,1,0:T(8,128)(2,1)S(1)}, bf16[1,16,64,2048]{3,2,1,0:T(8,128)(2,1)S(1)}) fusion(bf16[2,16,64,2048]{3,2,1,0:T(8,128)(2,1)} %get-tuple-element.10), kind=kLoop, calls=%fused_computation.43 | loop fusion | bytes 16777216 | tf_op jit(solution)/shard_map/slice | solution.py:519
  107.2 0.0 copy-start.1
  107.3 0.0 copy-start.3
  107.3 0.0 copy-done.4
  107.3 1.9 fusion.11
  109.2 0.0 copy-done.1
  109.2 0.0 copy-done
  109.2 0.0 copy-start.5
  109.2 0.0 copy-start.11
  109.2 1.9 fusion.8
  111.1 0.0 copy-start.7
  111.1 0.0 copy-done.3
  111.1 0.0 copy-done.5
  111.1 0.6 copy-done.11
  111.7 3.3 %multiply_reduce_fusion = (bf16[1024]{0:T(1024)(128)(2,1)S(1)}, bf16[1024,384]{0,1:T(8,128)(2,1)}, f32[1024,384]{0,1:T(8,128)}) fusion(f32[1024,384]{0,1:T(8,128)S(1)} %fusion.11, f32[1024,384]{0,1:T(8,128)S(1)} %fusion.8, bf16[1024,2048]{1,0:T(8,128)(2,1)S(1)} %bitcast.51, bf16[1,384,2048]{2,1,0:T(8,128)(2,1)S(1)} %copy-done.11), kind=kOutput, calls=%fused_computation.19 | convolution fusion | flops 1614150656 | bytes 11274240 | tf_op jit(solution)/shard_map/dot_general | solution.py:15
  115.0 0.0 copy-done.7
  115.0 0.1 reshape.34
  115.1 0.4 fusion.17
  115.5 0.1 mul.42
  115.6 0.0 copy-start.6
  115.6 0.0 copy-start.8
  115.6 5.6 %fusion.3 = bf16[1,384,2048]{2,1,0:T(8,128)(2,1)} fusion(bf16[1024,384]{0,1:T(8,128)(2,1)} %get-tuple-element.16, bf16[1024,2048]{1,0:T(8,128)(2,1)} %bitcast.52, f32[1024]{0:T(1024)S(1)} %mul.42), kind=kOutput, calls=%fused_computation.7 | convolution fusion | flops 1617690624 | bytes 6557696 | tf_op jit(solution)/shard_map/dot_general | solution.py:24
  121.2 0.0 copy-done.6
  121.2 0.0 copy-done.8
  121.2 0.0 copy-done.9
  121.2 0.0 copy-start.2
  121.2 1.0 multiply_convert_fusion.7
  122.2 1.2 copy-done.2
  123.4 3.6 %fusion.5 = bf16[1,2048,384]{2,1,0:T(8,128)(2,1)} fusion(bf16[1024,2048]{1,0:T(8,128)(2,1)S(1)} %bitcast.49, bf16[1024,384]{0,1:T(8,128)(2,1)S(1)} %get-tuple-element.19), kind=kOutput, calls=%fused_computation.9 | convolution fusion | flops 1611399168 | bytes 6553600 | tf_op jit(solution)/shard_map/dot_general | solution.py:28
  127.0 3.8 %fusion.4 = bf16[1,2048,384]{2,1,0:T(8,128)(2,1)} fusion(bf16[1024,2048]{1,0:T(8,128)(2,1)S(1)} %bitcast.50, bf16[1024,384]{0,1:T(8,128)(2,1)S(1)} %get-tuple-element.20), kind=kOutput, calls=%fused_computation.8 | convolution fusion | flops 1611399168 | bytes 6553600 | tf_op jit(solution)/shard_map/dot_general | solution.py:27
  130.8 2.4 %fusion.6 = f32[1024,2048]{1,0:T(8,128)S(1)} fusion(bf16[1024,384]{0,1:T(8,128)(2,1)S(1)} %get-tuple-element.20, bf16[1,2048,384]{2,1,0:T(8,128)(2,1)S(1)} %copy-done), kind=kOutput, calls=%fused_computation.10 | convolution fusion | flops 1610612736 | bytes 10747904 | tf_op jit(solution)/shard_map/dot_general | solution.py:30
  133.2 4.4 %add_convert_fusion = bf16[1024,2048]{1,0:T(8,128)(2,1)} fusion(f32[1024,2048]{1,0:T(8,128)S(1)} %fusion.6, bf16[1024,384]{0,1:T(8,128)(2,1)S(1)} %get-tuple-element.19, bf16[1,2048,384]{2,1,0:T(8,128)(2,1)S(1)} %copy-done.4), kind=kOutput, calls=%fused_computation.1 | convolution fusion | flops 1614807040 | bytes 14942208 | tf_op jit(solution)/shard_map/dot_general | solution.py:31
  137.6 0.6 broadcast_in_dim.82.gate_ref
  138.3 51.8 %shard_map.111 = (bf16[128,2048]{1,0:T(8,128)(2,1)}, f32[16,8,128]{2,1,0:T(8,128)}) custom-call(bf16[16,64,2048]{2,1,0:T(8,128)(2,1)} %bitcast.46, f32[16,8,128]{2,1,0:T(8,128)} %broadcast_in_dim.82.gate_ref, f32[16,16,128]{2,1,0:T(8,128)} %get-tuple-element.9.metas), custom_call_target="tpu_custom_call" | custom-call | tf_op jit(solution)/shard_map/pallas_call | solution.py:528
  190.1 0.8 slice.11
  190.9 0.0 copy-done.10
  190.9 0.5 select_reduce_fusion
  191.5 1.9 copy.13
  (4 shorter events, 0.0 us)
Async XLA Ops:
  0.6 108.5 %copy-start = (bf16[1,2048,384]{2,1,0:T(8,128)(2,1)S(1)}, bf16[1,2048,384]{2,1,0:T(8,128)(2,1)}, u32[]{:S(2)}) copy-start(bf16[1,2048,384]{2,1,0:T(8,128)(2,1)} %param.11) | copy-start | bytes 4718596
  102.9 4.3 %copy-start.4 = (bf16[1,2048,384]{2,1,0:T(8,128)(2,1)S(1)}, bf16[1,2048,384]{2,1,0:T(8,128)(2,1)}, u32[]{:S(2)}) copy-start(bf16[1,2048,384]{2,1,0:T(8,128)(2,1)} %param.12) | copy-start | bytes 4718596
  107.2 1.9 copy-start.1
  107.3 3.9 %copy-start.3 = (bf16[1,16,64,2048]{3,2,1,0:T(8,128)(2,1)}, bf16[1,16,64,2048]{3,2,1,0:T(8,128)(2,1)S(1)}, u32[]{:S(2)}) copy-start(bf16[1,16,64,2048]{3,2,1,0:T(8,128)(2,1)S(1)} %get-tuple-element.17) | copy-start | bytes 12582916
  109.2 1.9 %copy-start.5 = (f32[1024,384]{0,1:T(8,128)}, f32[1024,384]{0,1:T(8,128)S(1)}, u32[]{:S(2)}) copy-start(f32[1024,384]{0,1:T(8,128)S(1)} %fusion.11) | copy-start | bytes 4718596
  109.2 2.5 %copy-start.11 = (bf16[1,384,2048]{2,1,0:T(8,128)(2,1)S(1)}, bf16[1,384,2048]{2,1,0:T(8,128)(2,1)}, u32[]{:S(2)}) copy-start(bf16[1,384,2048]{2,1,0:T(8,128)(2,1)} %param.13) | copy-start | bytes 4718596
  111.1 3.9 %copy-start.7 = (f32[1024,384]{0,1:T(8,128)}, f32[1024,384]{0,1:T(8,128)S(1)}, u32[]{:S(2)}) copy-start(f32[1024,384]{0,1:T(8,128)S(1)} %fusion.8) | copy-start | bytes 4718596
  115.6 5.6 %copy-start.6 = (f32[1024,384]{0,1:T(8,128)S(1)}, f32[1024,384]{0,1:T(8,128)}, u32[]{:S(2)}) copy-start(f32[1024,384]{0,1:T(8,128)} %copy-done.5) | copy-start | bytes 4718596
  115.6 5.6 %copy-start.8 = (f32[1024,384]{0,1:T(8,128)S(1)}, f32[1024,384]{0,1:T(8,128)}, u32[]{:S(2)}) copy-start(f32[1024,384]{0,1:T(8,128)} %copy-done.7) | copy-start | bytes 4718596
  115.6 5.6 %copy-start.9 = (f32[1024,384]{0,1:T(8,128)S(1)}, f32[1024,384]{0,1:T(8,128)}, u32[]{:S(2)}) copy-start(f32[1024,384]{0,1:T(8,128)} %get-tuple-element.23) | copy-start | bytes 4718596
  121.2 2.2 %copy-start.2 = (bf16[1,16,64,2048]{3,2,1,0:T(8,128)(2,1)S(1)}, bf16[1,16,64,2048]{3,2,1,0:T(8,128)(2,1)}, u32[]{:S(2)}) copy-start(bf16[1,16,64,2048]{3,2,1,0:T(8,128)(2,1)} %copy-done.1) | copy-start | bytes 12582916
  138.3 52.7 %copy-start.10 = (s32[128,2]{0,1:T(2,128)S(1)}, s32[128,2]{0,1:T(2,128)}, u32[]{:S(2)}) copy-start(s32[128,2]{0,1:T(2,128)} %param.10) | copy-start | bytes 3076

commit v2 on v0

--- a/solution.py
+++ b/solution.py
@@ -1,6 +1,8 @@
 import jax
 import jax.numpy as jnp
 from jax import lax
+from jax.experimental import pallas as pl
+from jax.experimental.pallas import tpu as pltpu
 from jax.sharding import PartitionSpec as P
 
 
@@ -118,6 +120,467 @@
     return (token_grad, prob_grad, gate_grad[None], up_grad[None], down_grad[None])
 
 
+NZ, NY, NC = 4, 2, 2
+NS = NZ * NY * NC
+COLS = 512
+TILE = 256
+LIMIT = 56 * 2**20
+
+
+def place_of(index):
+    return index // (NY * NC), (index // NC) % NY, index % NC
+
+
+def index_of(z, y, c):
+    return z * (NY * NC) + y * NC + c
+
+
+def enter(me):
+    barrier = pltpu.get_barrier_semaphore()
+
+    def greet(i, carry):
+        pl.semaphore_signal(
+            barrier, inc=1, device_id={"expert": (me + i) % NS}, device_id_type=pl.DeviceIdType.MESH
+        )
+        return carry
+
+    lax.fori_loop(1, NS, greet, 0)
+    pl.semaphore_wait(barrier, NS - 1)
+
+
+def remote(src, dst, send, recv, target):
+    return pltpu.make_async_remote_copy(
+        src_ref=src,
+        dst_ref=dst,
+        send_sem=send,
+        recv_sem=recv,
+        device_id={"expert": target},
+        device_id_type=pl.DeviceIdType.MESH,
+    )
+
+
+def onehot_rows(metas, source, own, other, cap):
+    slot = lax.broadcasted_iota(jnp.int32, (cap, metas.shape[2]), 0).astype(jnp.float32)
+    mine = metas[source, pl.ds(own, 1), :]
+    theirs = metas[source, pl.ds(other, 1), :]
+    return jnp.concatenate([slot == mine, slot == theirs], axis=0).astype(jnp.bfloat16)
+
+
+def fused_kernel(
+    x_ref, g_ref, meta_ref, wg_ref, wu_ref, wd_ref,
+    token_ref, gates, gate_out, up_out, down_out,
+    metas, zbuf, ysend, slots, wgu, wd, gpu, hid_t, prob, part, gout, half, pairs, dense, came,
+    loc_sem, meta_send, meta_recv, up_send, dn_send, z_recv, y_send, y_recv, c_send, c_recv,
+    h_send, h_recv, q_send, q_recv, p_send, p_recv, r_send, r_recv,
+):
+    me = lax.axis_index("expert")
+    z, y, c = place_of(me)
+    own, other = z * NY + y, z * NY + (1 - y)
+    experts = NS // 2
+    cap, width = slots.shape[2], slots.shape[3]
+    hidden = wd.shape[0]
+    column = NY * NC
+    rows_col = column * cap
+    pieces = width // COLS
+    loads = (
+        pltpu.make_async_copy(x_ref, zbuf.at[z, 0], loc_sem.at[0]),
+        pltpu.make_async_copy(g_ref, zbuf.at[z, 1], loc_sem.at[1]),
+        pltpu.make_async_copy(wg_ref, wgu.at[:, pl.ds(0, hidden)], loc_sem.at[2]),
+        pltpu.make_async_copy(wu_ref, wgu.at[:, pl.ds(hidden, hidden)], loc_sem.at[3]),
+        pltpu.make_async_copy(wd_ref, wd, loc_sem.at[4]),
+    )
+    for load in loads:
+        load.start()
+    metas[me] = meta_ref[...]
+    enter(me)
+
+    def meta_copy(source, target):
+        return remote(metas.at[source], metas.at[source], meta_send.at[target], meta_recv.at[source], target)
+
+    def up_copy(zz, a):
+        return remote(
+            zbuf.at[zz, a], zbuf.at[zz, a], up_send.at[zz, a], z_recv.at[zz, a], index_of(z + 1, y, c)
+        )
+
+    def dn_copy(zz, a):
+        return remote(
+            zbuf.at[zz, a], zbuf.at[zz, a], dn_send.at[zz, a], z_recv.at[zz, a], index_of(z - 1, y, c)
+        )
+
+    def y_copy(zz, a):
+        return remote(
+            ysend.at[a, zz],
+            slots.at[a, index_of(zz, y, c)],
+            y_send.at[a, zz],
+            y_recv.at[a, zz],
+            index_of(z, 1 - y, c),
+        )
+
+    def c_copy(source, a):
+        return remote(
+            slots.at[a, source],
+            slots.at[a, source],
+            c_send.at[a, source],
+            c_recv.at[a, source],
+            index_of(z, y, 1 - c),
+        )
+
+    def h_copy(zz, yy):
+        return remote(
+            part.at[index_of(zz, yy, 1 - c)],
+            half.at[zz, yy],
+            h_send.at[zz, yy],
+            h_recv.at[zz, yy],
+            index_of(z, y, 1 - c),
+        )
+
+    def q_copy(target):
+        return remote(gout.at[target], gates.at[me], q_send.at[target], q_recv.at[me], target)
+
+    def p_copy(zz):
+        return remote(
+            pairs.at[zz, 2], pairs.at[zz, 1], p_send.at[zz], p_recv.at[zz], index_of(z, 1 - y, c)
+        )
+
+    def r_copy(zz, way, j):
+        return remote(
+            dense.at[zz, j],
+            came.at[zz, way, j],
+            r_send.at[zz, j],
+            r_recv.at[zz, way, j],
+            index_of(z - 1 + 2 * way, y, c),
+        )
+
+    def arrived(ref, sem):
+        pltpu.make_async_copy(ref, ref, sem).wait()
+
+    def both_ways(d, fn):
+        @pl.loop(0, 2)
+        def _(way):
+            zz = z - d + 2 * d * way
+            pl.when((zz >= 0) & (zz < NZ) & ((d > 0) | (way == 0)))(lambda: fn(zz))
+
+    def forward(zz, a):
+        @pl.when((zz <= z) & (z < NZ - 1))
+        def _():
+            up_copy(zz, a).start()
+
+        @pl.when((zz >= z) & (z > 0))
+        def _():
+            dn_copy(zz, a).start()
+
+    def pick(zz, a):
+        source = index_of(zz, y, c)
+        hot = onehot_rows(metas, source, own, other, cap)
+
+        @pl.loop(0, pieces)
+        def _(j):
+            cols = pl.ds(pl.multiple_of(j * COLS, COLS), COLS)
+            rows = jnp.dot(hot, zbuf[zz, a, :, cols], preferred_element_type=jnp.float32)
+            rows = rows.astype(jnp.bfloat16)
+            slots[a, source, :, cols] = rows[:cap]
+            ysend[a, zz, :, cols] = rows[cap:]
+
+        y_copy(zz, a).start()
+        c_copy(source, a).start()
+
+    def relay(zz, a):
+        source = index_of(zz, 1 - y, c)
+        arrived(slots.at[a, source], y_recv.at[a, zz])
+        c_copy(source, a).start()
+
+    def block(zz):
+        base = zz * column
+        hots = []
+        probs = []
+        for i in range(column):
+            row = metas[base + i, pl.ds(own, 1), :]
+            slot = lax.broadcasted_iota(jnp.int32, (cap, row.shape[1]), 0).astype(jnp.float32)
+            hots.append(slot == row)
+            weight = metas[base + i, pl.ds(own + experts, 1), :]
+            probs.append(jnp.sum(jnp.where(hots[i], weight, 0.0), axis=1, keepdims=True))
+        p = jnp.concatenate(probs, axis=0)
+        prob[zz] = p
+        rows_x = slots[0, pl.ds(base, column)].reshape(rows_col, width)
+        pre = jnp.dot(rows_x, wgu[...], preferred_element_type=jnp.float32)
+        pre_gate, pre_up = pre[:, :hidden], pre[:, hidden:]
+        rows_g = slots[1, pl.ds(base, column)].reshape(rows_col, width)
+        back = lax.dot_general(
+            rows_g, wd[...], (((1,), (1,)), ((), ())), preferred_element_type=jnp.float32
+        )
+        sigma = jax.nn.sigmoid(pre_gate)
+        active = pre_gate * sigma
+        hid = (active * pre_up).astype(jnp.bfloat16)
+        q = jnp.sum(back * hid.astype(jnp.float32), axis=1, keepdims=True)
+        q = q.astype(jnp.bfloat16).astype(jnp.float32)
+        scaled = p * back
+        gpu[zz, :, :hidden] = (
+            scaled * pre_up * sigma * (1.0 + pre_gate * (1.0 - sigma))
+        ).astype(jnp.bfloat16)
+        gpu[zz, :, hidden:] = (scaled * active).astype(jnp.bfloat16)
+        hid_t[zz] = hid.T
+        for i in range(column):
+            gate = jnp.sum(jnp.where(hots[i], q[i * cap : (i + 1) * cap], 0.0), axis=0, keepdims=True)
+            gout[base + i] = jnp.broadcast_to(gate, gout.shape[1:])
+
+        @pl.loop(0, pieces)
+        def _(j):
+            cols = pl.ds(pl.multiple_of(j * COLS, COLS), COLS)
+            grads = lax.dot_general(
+                gpu[zz], wgu[cols, :], (((1,), (1,)), ((), ())), preferred_element_type=jnp.float32
+            )
+            part[pl.ds(base, column), :, cols] = grads.astype(jnp.bfloat16).reshape(column, cap, COLS)
+
+    def add_half(zz, yy, to):
+        source = index_of(zz, yy, c)
+        h_copy(zz, yy).wait_recv()
+
+        @pl.loop(0, pieces)
+        def _(j):
+            cols = pl.ds(pl.multiple_of(j * COLS, COLS), COLS)
+            pairs[zz, to, :, cols] = (
+                part[source, :, cols].astype(jnp.float32) + half[zz, yy, :, cols].astype(jnp.float32)
+            ).astype(jnp.bfloat16)
+
+    def gate_row(i, fn):
+        pl.when(i != me)(lambda: fn(i))
+
+    def spread(zz, j):
+        cols = pl.ds(pl.multiple_of(j * COLS, COLS), COLS)
+        hot = onehot_rows(metas, index_of(zz, y, c), own, other, cap)
+        rows = jnp.concatenate([pairs[zz, 0, :, cols], pairs[zz, 1, :, cols]], axis=0)
+        total = lax.dot_general(hot, rows, (((0,), (0,)), ((), ())), preferred_element_type=jnp.float32)
+        return total.astype(jnp.bfloat16)
+
+    def add_came(value, zz, way, j):
+        arrived(came.at[zz, way, j], r_recv.at[zz, way, j])
+        return (value.astype(jnp.float32) + came[zz, way, j].astype(jnp.float32)).astype(jnp.bfloat16)
+
+    def chain(zz, relayed):
+        way = jnp.where(zz < z, 0, 1)
+        p_copy(zz).wait_recv()
+
+        @pl.loop(0, pieces)
+        def _(j):
+            value = spread(zz, j)
+            dense[zz, j] = add_came(value, zz, way, j) if relayed else value
+            r_copy(zz, way, j).start()
+
+    middle = (z > 0) & (z < NZ - 1)
+
+    def process(zz):
+        for a in range(2):
+            relay(zz, a)
+        for a in range(2):
+            for yy in range(NY):
+                c_copy(index_of(zz, yy, 1 - c), a).wait_recv()
+        block(zz)
+        for i in range(NY):
+            h_copy(zz, (1 - y + i) % NY).start()
+        for i in range(column):
+            gate_row(zz * column + i, lambda target: q_copy(target).start())
+        add_half(zz, 1 - y, 2)
+        p_copy(zz).start()
+        add_half(zz, y, 0)
+        pl.when(jnp.logical_not(middle) & (zz != z))(lambda: chain(zz, False))
+
+    loads[0].wait()
+    forward(z, 0)
+    loads[1].wait()
+    forward(z, 1)
+
+    def give_meta(i, carry):
+        meta_copy(me, (me + i) % NS).start()
+        return carry
+
+    def take_meta(i, carry):
+        source = (me + i) % NS
+        meta_copy(source, source).wait_recv()
+        return carry
+
+    lax.fori_loop(1, NS, give_meta, 0)
+    lax.fori_loop(1, NS, take_meta, 0)
+
+    @pl.loop(0, NZ)
+    def _(d):
+        for a in range(2):
+
+            def step(zz, a=a):
+                @pl.when(d > 0)
+                def _():
+                    arrived(zbuf.at[zz, a], z_recv.at[zz, a])
+                    forward(zz, a)
+
+                pick(zz, a)
+
+            both_ways(d, step)
+
+        @pl.when(d == 0)
+        def _():
+            for load in loads[2:]:
+                load.wait()
+
+        both_ways(d, process)
+
+    @pl.loop(0, width // TILE)
+    def _(j):
+        cols = pl.ds(pl.multiple_of(j * TILE, TILE), TILE)
+        wide = jnp.zeros((TILE, 2 * hidden), jnp.float32)
+        down = jnp.zeros((hidden, TILE), jnp.float32)
+        for k in range(NZ):
+            rows_x = slots[0, k * column : (k + 1) * column, :, cols].reshape(rows_col, TILE)
+            wide += lax.dot_general(
+                rows_x, gpu[k], (((0,), (0,)), ((), ())), preferred_element_type=jnp.float32
+            )
+            rows_g = slots[1, k * column : (k + 1) * column, :, cols].reshape(rows_col, TILE)
+            scaled = (prob[k] * rows_g.astype(jnp.float32)).astype(jnp.bfloat16)
+            down += jnp.dot(hid_t[k], scaled, preferred_element_type=jnp.float32)
+        gate_out[cols, :] = wide[:, :hidden].astype(jnp.bfloat16)
+        up_out[cols, :] = wide[:, hidden:].astype(jnp.bfloat16)
+        down_out[:, cols] = down.astype(jnp.bfloat16)
+
+    @pl.when(middle)
+    def _():
+        long_side = 1 - 2 * (z // 2)
+        for i in range(NZ - 2):
+            chain(z + long_side * (i + 1), True)
+        chain(z - long_side, True)
+
+    p_copy(z).wait_recv()
+
+    @pl.loop(0, pieces)
+    def _(j):
+        cols = pl.ds(pl.multiple_of(j * COLS, COLS), COLS)
+        token_ref[:, cols] = spread(z, j)
+
+        @pl.when(z < NZ - 1)
+        def _():
+            token_ref[:, cols] = add_came(token_ref[:, cols], z, 0, j)
+
+        @pl.when(z > 0)
+        def _():
+            token_ref[:, cols] = add_came(token_ref[:, cols], z, 1, j)
+
+    gates[me] = gout[me]
+
+    def finish(zz, carry):
+        for a in range(2):
+
+            @pl.when((zz <= z) & (z < NZ - 1))
+            def _():
+                up_copy(zz, a).wait_send()
+
+            @pl.when((zz >= z) & (z > 0))
+            def _():
+                dn_copy(zz, a).wait_send()
+
+            y_copy(zz, a).wait_send()
+            for yy in range(NY):
+                c_copy(index_of(zz, yy, c), a).wait_send()
+        for yy in range(NY):
+            h_copy(zz, yy).wait_send()
+        p_copy(zz).wait_send()
+
+        @pl.when(zz != z)
+        def _():
+            for j in range(pieces):
+                r_copy(zz, jnp.where(zz < z, 0, 1), j).wait_send()
+
+        return carry
+
+    lax.fori_loop(0, NZ, finish, 0)
+
+    def done(i, carry):
+        target = (me + i) % NS
+        meta_copy(me, target).wait_send()
+        q_copy(target).wait_send()
+        arrived(gates.at[target], q_recv.at[target])
+        return carry
+
+    lax.fori_loop(1, NS, done, 0)
+
+
+def route_tables(route_probs, expert_ids, experts):
+    tok_count = expert_ids.shape[0]
+    names = jnp.arange(experts, dtype=jnp.int32)
+    hit = expert_ids.T[:, None, :] == names[None, :, None]
+    routed = jnp.any(hit, axis=0)
+    order = jnp.arange(tok_count, dtype=jnp.int32)
+    before = (order[:, None] < order[None, :]).astype(jnp.bfloat16)
+    rank = jnp.dot(routed.astype(jnp.bfloat16), before, preferred_element_type=jnp.float32)
+    slot = jnp.where(routed, rank, -1.0)
+    prob = jnp.sum(jnp.where(hit, route_probs.T.astype(jnp.float32)[:, None, :], 0.0), axis=0)
+    return hit, jnp.concatenate([slot, prob], axis=0)
+
+
+def local_chips(tokens, cotangent, route_probs, expert_ids, w_gate, w_up, w_down):
+    tok_count, d_model = tokens.shape
+    per_token = expert_ids.shape[1]
+    experts = NS // 2
+    cap = 2 * (tok_count * per_token // experts)
+    hit, meta = route_tables(route_probs, expert_ids, experts)
+    hidden = w_down.shape[1]
+    column = NY * NC
+    pieces = d_model // COLS
+    vmem = pl.BlockSpec(memory_space=pltpu.VMEM)
+    hbm = pl.BlockSpec(memory_space=pl.ANY)
+    dma = pltpu.SemaphoreType.DMA
+    half_type = jnp.bfloat16
+    token_grad, gates, gate_grad, up_grad, down_grad = pl.pallas_call(
+        fused_kernel,
+        out_shape=(
+            jax.ShapeDtypeStruct((tok_count, d_model), half_type),
+            jax.ShapeDtypeStruct((NS, 8, tok_count), jnp.float32),
+            jax.ShapeDtypeStruct((d_model, hidden), half_type),
+            jax.ShapeDtypeStruct((d_model, hidden), half_type),
+            jax.ShapeDtypeStruct((hidden, d_model), half_type),
+        ),
+        in_specs=[hbm, hbm, vmem, hbm, hbm, hbm],
+        out_specs=(vmem,) * 5,
+        scratch_shapes=[
+            pltpu.VMEM((NS,) + meta.shape, jnp.float32),
+            pltpu.VMEM((NZ, 2, tok_count, d_model), half_type),
+            pltpu.VMEM((2, NZ, cap, d_model), half_type),
+            pltpu.VMEM((2, NS, cap, d_model), half_type),
+            pltpu.VMEM((d_model, 2 * hidden), half_type),
+            pltpu.VMEM((hidden, d_model), half_type),
+            pltpu.VMEM((NZ, column * cap, 2 * hidden), half_type),
+            pltpu.VMEM((NZ, hidden, column * cap), half_type),
+            pltpu.VMEM((NZ, column * cap, 1), jnp.float32),
+            pltpu.VMEM((NS, cap, d_model), half_type),
+            pltpu.VMEM((NS, 8, tok_count), jnp.float32),
+            pltpu.VMEM((NZ, NY, cap, d_model), half_type),
+            pltpu.VMEM((NZ, 3, cap, d_model), half_type),
+            pltpu.VMEM((NZ, pieces, tok_count, COLS), half_type),
+            pltpu.VMEM((NZ, 2, pieces, tok_count, COLS), half_type),
+            dma((5,)),
+            dma((NS,)),
+            dma((NS,)),
+            dma((NZ, 2)),
+            dma((NZ, 2)),
+            dma((NZ, 2)),
+            dma((2, NZ)),
+            dma((2, NZ)),
+            dma((2, NS)),
+            dma((2, NS)),
+            dma((NZ, NY)),
+            dma((NZ, NY)),
+            dma((NS,)),
+            dma((NS,)),
+            dma((NZ,)),
+            dma((NZ,)),
+            dma((NZ, pieces)),
+            dma((NZ, 2, pieces)),
+        ],
+        compiler_params=pltpu.CompilerParams(
+            collective_id=0, has_side_effects=True, vmem_limit_bytes=LIMIT
+        ),
+    )(tokens, cotangent, meta, w_gate[0], w_up[0], w_down[0])
+    both = gates[:, 0, :].reshape(experts, 2, tok_count).sum(axis=1)
+    prob_grad = jnp.sum(jnp.where(hit, both[None], 0.0), axis=1).T.astype(jnp.bfloat16)
+    return (token_grad, prob_grad, gate_grad[None], up_grad[None], down_grad[None])
+
+
 def solution(mesh):
     in_specs = (
         P(("groups", "expert"), None),
@@ -135,4 +598,5 @@
         P(("groups", "expert"), None, None),
         P(("groups", "expert"), None, None),
     )
-    return jax.shard_map(local, mesh=mesh, in_specs=in_specs, out_specs=out_specs, check_vma=False)
+    body = local_chips if mesh.shape["expert"] == NS else local
+    return jax.shard_map(body, mesh=mesh, in_specs=in_specs, out_specs=out_specs, check_vma=False)

time: 362 us -> 177 us (0.49)
  the two profiles are of different devices: /device:TPU:15 before, /device:TPU:0 now
where the time goes in v2:
time: 177 us
  Pallas kernels  164 us (93%)
  local copies, waits for them, and re-layouts  8.68 us (5%)
  other arithmetic  3.18 us (2%)
    pallas_call x1, Pallas kernels, local_chips(): pl.pallas_call(fused_kernel, out_shape=(jax.ShapeDtypeStruct((tok_count,...  164 us
    unnamed x10, local copies, waits for them, and re-layouts  7.83 us

profile of v2, /device:TPU:0, one launch (start us, length us, event | category | flops | bytes accessed | tf_op | source)
XLA Modules:
  0.0 176.5 jit_solution(9137537051217576730)
XLA Ops:
  0.6 0.7 convert_bitcast_fusion
  1.3 0.7 fusion
  2.0 0.1 convolution_select_fusion
  2.1 0.7 select_reduce_fusion.1
  2.8 0.6 pad_maximum_fusion.meta_ref
  3.4 0.0 copy-start.2
  3.4 163.9 %shard_map.110 = (bf16[128,2048]{1,0:T(8,128)(2,1)}, f32[16,8,128]{2,1,0:T(8,128)}, bf16[2048,384]{1,0:T(8,128)(2,1)}, bf16[2048,384]{1,0:T(8,128)(2,1)}, bf16[384,2048]{1,0:T(8,128)(2,1)}) custom-call(bf16[128,2048]{1,0:T(8,128)(2,1)} %x_ref.1, bf16[128,2048]{1,0:T(8,128)(2,1)} %g_ref.1, f32[16,128]{1,0:T(8,128)} %pad_maximum_fusion.meta_ref, ...), custom_call_target="tpu_custom_call" | custom-call | tf_op jit(solution)/shard_map/pallas_call | solution.py:529
  167.3 0.8 slice.3
  168.1 0.0 copy-done.2
  168.1 0.5 select_reduce_fusion
  168.7 1.9 %copy.16 = bf16[128,2048]{1,0:T(8,128)(2,1)} copy(bf16[128,2048]{1,0:T(8,128)(2,1)} %get-tuple-element.20) | data formatting | bytes 1048576
  170.6 0.0 copy-start.1
  170.6 2.8 %copy.17 = bf16[1,2048,384]{2,1,0:T(8,128)(2,1)} copy(bf16[1,2048,384]{2,1,0:T(8,128)(2,1)} %bitcast.16) | data formatting | bytes 3145728
  173.4 0.0 copy-done.1
  173.4 0.0 copy-start
  173.4 1.1 copy.18
  174.5 0.8 copy-done
  175.4 1.1 copy.19
  (1 shorter events, 0.0 us)
Async XLA Ops:
  3.4 164.7 %copy-start.2 = (s32[128,2]{0,1:T(2,128)S(1)}, s32[128,2]{0,1:T(2,128)}, u32[]{:S(2)}) copy-start(s32[128,2]{0,1:T(2,128)} %param.10) | copy-start | bytes 3076
  170.6 2.8 %copy-start.1 = (bf16[2048,384]{1,0:T(8,128)(2,1)S(1)}, bf16[2048,384]{1,0:T(8,128)(2,1)}, u32[]{:S(2)}) copy-start(bf16[2048,384]{1,0:T(8,128)(2,1)} %get-tuple-element.13) | copy-start | bytes 4718596
  173.4 2.0 %copy-start = (bf16[384,2048]{1,0:T(8,128)(2,1)S(1)}, bf16[384,2048]{1,0:T(8,128)(2,1)}, u32[]{:S(2)}) copy-start(bf16[384,2048]{1,0:T(8,128)(2,1)} %get-tuple-element.14) | copy-start | bytes 4718596

commit v3 on v2

--- a/solution.py
+++ b/solution.py
@@ -122,7 +122,7 @@
 
 NZ, NY, NC = 4, 2, 2
 NS = NZ * NY * NC
-COLS = 512
+COLS = 1024
 TILE = 256
 LIMIT = 56 * 2**20
 
@@ -382,12 +382,17 @@
         add_half(zz, 1 - y, 2)
         p_copy(zz).start()
         add_half(zz, y, 0)
-        pl.when(jnp.logical_not(middle) & (zz != z))(lambda: chain(zz, False))
+
+    long_side = 1 - 2 * (z // 2)
+
+    def send_own_g(side):
+        pl.when((side == 1) & (z < NZ - 1))(lambda: up_copy(z, 1).start())
+        pl.when((side == -1) & (z > 0))(lambda: dn_copy(z, 1).start())
 
     loads[0].wait()
     forward(z, 0)
     loads[1].wait()
-    forward(z, 1)
+    pl.when(jnp.logical_not(middle))(lambda: send_own_g(long_side))
 
     def give_meta(i, carry):
         meta_copy(me, (me + i) % NS).start()
@@ -403,24 +408,41 @@
 
     @pl.loop(0, NZ)
     def _(d):
-        for a in range(2):
-
-            def step(zz, a=a):
-                @pl.when(d > 0)
-                def _():
-                    arrived(zbuf.at[zz, a], z_recv.at[zz, a])
-                    forward(zz, a)
-
-                pick(zz, a)
-
-            both_ways(d, step)
-
-        @pl.when(d == 0)
+        def step(zz):
+            @pl.when(d > 0)
+            def _():
+                arrived(zbuf.at[zz, 0], z_recv.at[zz, 0])
+                forward(zz, 0)
+
+            pick(zz, 0)
+
+        both_ways(d, step)
+
+    pick(z, 1)
+    for load in loads[2:]:
+        load.wait()
+
+    @pl.loop(0, NZ)
+    def _(k):
+        come = z + long_side * jnp.where(middle, jnp.where(k == 0, -1, NZ - 1 - k), NZ - k)
+
+        @pl.when((middle & (k < NZ - 1)) | (jnp.logical_not(middle) & (k > 0)))
         def _():
-            for load in loads[2:]:
-                load.wait()
-
-        both_ways(d, process)
+            arrived(zbuf.at[come, 1], z_recv.at[come, 1])
+            forward(come, 1)
+            pl.when(middle & (k == 0))(lambda: send_own_g(long_side))
+            pl.when(middle & (k == NZ - 2))(lambda: send_own_g(-long_side))
+            pick(come, 1)
+
+        pl.when(jnp.logical_not(middle) & (k > 1))(lambda: chain(z + long_side * (NZ + 1 - k), False))
+        process(z + long_side * jnp.where(k == 0, 0, jnp.where(middle & (k == 1), -1, NZ - k)))
+
+    pl.when(jnp.logical_not(middle))(lambda: chain(z + long_side, False))
+
+    @pl.when(middle)
+    def _():
+        chain(z + 2 * long_side, True)
+        chain(z - long_side, True)
 
     @pl.loop(0, width // TILE)
     def _(j):
@@ -441,10 +463,7 @@
 
     @pl.when(middle)
     def _():
-        long_side = 1 - 2 * (z // 2)
-        for i in range(NZ - 2):
-            chain(z + long_side * (i + 1), True)
-        chain(z - long_side, True)
+        chain(z + long_side, True)
 
     p_copy(z).wait_recv()
 

time: 177 us -> 167 us (0.944)
  Pallas kernels: 164 us -> 154 us
    pallas_call x1, Pallas kernels: 164 us -> 154 us  [local_chips(): pl.pallas_call(fused_kernel, out_shape=(jax.ShapeDtypeStruct((tok_count,...]
where the time goes in v3:
time: 167 us
  Pallas kernels  154 us (92%)
  local copies, waits for them, and re-layouts  8.68 us (5%)
  other arithmetic  3.18 us (2%)
    pallas_call x1, Pallas kernels, local_chips(): pl.pallas_call(fused_kernel, out_shape=(jax.ShapeDtypeStruct((tok_count,...  154 us
    unnamed x10, local copies, waits for them, and re-layouts  7.83 us

profile of v3, /device:TPU:0, one launch (start us, length us, event | category | flops | bytes accessed | tf_op | source)
XLA Modules:
  0.0 166.6 jit_solution(6776253888015579866)
XLA Ops:
  0.6 0.7 convert_bitcast_fusion
  1.3 0.7 fusion
  2.0 0.1 convolution_select_fusion
  2.1 0.7 select_reduce_fusion.1
  2.8 0.6 pad_maximum_fusion.meta_ref
  3.4 0.0 copy-start.2
  3.4 153.9 %shard_map.110 = (bf16[128,2048]{1,0:T(8,128)(2,1)}, f32[16,8,128]{2,1,0:T(8,128)}, bf16[2048,384]{1,0:T(8,128)(2,1)}, bf16[2048,384]{1,0:T(8,128)(2,1)}, bf16[384,2048]{1,0:T(8,128)(2,1)}) custom-call(bf16[128,2048]{1,0:T(8,128)(2,1)} %x_ref.1, bf16[128,2048]{1,0:T(8,128)(2,1)} %g_ref.1, f32[16,128]{1,0:T(8,128)} %pad_maximum_fusion.meta_ref, ...), custom_call_target="tpu_custom_call" | custom-call | tf_op jit(solution)/shard_map/pallas_call | solution.py:548
  157.3 0.8 slice.3
  158.2 0.0 copy-done.2
  158.2 0.5 select_reduce_fusion
  158.7 1.9 %copy.16 = bf16[128,2048]{1,0:T(8,128)(2,1)} copy(bf16[128,2048]{1,0:T(8,128)(2,1)} %get-tuple-element.20) | data formatting | bytes 1048576
  160.6 0.0 copy-start.1
  160.6 2.8 %copy.17 = bf16[1,2048,384]{2,1,0:T(8,128)(2,1)} copy(bf16[1,2048,384]{2,1,0:T(8,128)(2,1)} %bitcast.16) | data formatting | bytes 3145728
  163.4 0.0 copy-done.1
  163.4 0.0 copy-start
  163.4 1.1 copy.18
  164.6 0.8 copy-done
  165.4 1.1 copy.19
  (1 shorter events, 0.0 us)
Async XLA Ops:
  3.4 154.8 %copy-start.2 = (s32[128,2]{0,1:T(2,128)S(1)}, s32[128,2]{0,1:T(2,128)}, u32[]{:S(2)}) copy-start(s32[128,2]{0,1:T(2,128)} %param.10) | copy-start | bytes 3076
  160.6 2.8 %copy-start.1 = (bf16[2048,384]{1,0:T(8,128)(2,1)S(1)}, bf16[2048,384]{1,0:T(8,128)(2,1)}, u32[]{:S(2)}) copy-start(bf16[2048,384]{1,0:T(8,128)(2,1)} %get-tuple-element.13) | copy-start | bytes 4718596
  163.4 2.0 %copy-start = (bf16[384,2048]{1,0:T(8,128)(2,1)S(1)}, bf16[384,2048]{1,0:T(8,128)(2,1)}, u32[]{:S(2)}) copy-start(bf16[384,2048]{1,0:T(8,128)(2,1)} %get-tuple-element.14) | copy-start | bytes 4718596

commit v4 on v3

--- a/solution.py
+++ b/solution.py
@@ -123,6 +123,7 @@
 NZ, NY, NC = 4, 2, 2
 NS = NZ * NY * NC
 COLS = 1024
+WIDE = 2048
 TILE = 256
 LIMIT = 56 * 2**20
 
@@ -273,9 +274,9 @@
         source = index_of(zz, y, c)
         hot = onehot_rows(metas, source, own, other, cap)
 
-        @pl.loop(0, pieces)
+        @pl.loop(0, width // WIDE)
         def _(j):
-            cols = pl.ds(pl.multiple_of(j * COLS, COLS), COLS)
+            cols = pl.ds(pl.multiple_of(j * WIDE, WIDE), WIDE)
             rows = jnp.dot(hot, zbuf[zz, a, :, cols], preferred_element_type=jnp.float32)
             rows = rows.astype(jnp.bfloat16)
             slots[a, source, :, cols] = rows[:cap]
@@ -335,9 +336,9 @@
         source = index_of(zz, yy, c)
         h_copy(zz, yy).wait_recv()
 
-        @pl.loop(0, pieces)
+        @pl.loop(0, width // WIDE)
         def _(j):
-            cols = pl.ds(pl.multiple_of(j * COLS, COLS), COLS)
+            cols = pl.ds(pl.multiple_of(j * WIDE, WIDE), WIDE)
             pairs[zz, to, :, cols] = (
                 part[source, :, cols].astype(jnp.float32) + half[zz, yy, :, cols].astype(jnp.float32)
             ).astype(jnp.bfloat16)

time: 167 us -> 166 us (level)
  no operation moved by 1% of the time
where the time goes in v4:
time: 166 us
  Pallas kernels  153 us (92%)
  local copies, waits for them, and re-layouts  8.68 us (5%)
  other arithmetic  3.18 us (2%)
    pallas_call x1, Pallas kernels, local_chips(): pl.pallas_call(fused_kernel, out_shape=(jax.ShapeDtypeStruct((tok_count,...  153 us
    unnamed x10, local copies, waits for them, and re-layouts  7.83 us

profile of v4, /device:TPU:0, one launch (start us, length us, event | category | flops | bytes accessed | tf_op | source)
XLA Modules:
  0.0 166.0 jit_solution(6572076464148797942)
XLA Ops:
  0.6 0.7 convert_bitcast_fusion
  1.3 0.7 fusion
  2.0 0.1 convolution_select_fusion
  2.1 0.7 select_reduce_fusion.1
  2.8 0.6 pad_maximum_fusion.meta_ref
  3.4 0.0 copy-start.2
  3.4 153.4 %shard_map.110 = (bf16[128,2048]{1,0:T(8,128)(2,1)}, f32[16,8,128]{2,1,0:T(8,128)}, bf16[2048,384]{1,0:T(8,128)(2,1)}, bf16[2048,384]{1,0:T(8,128)(2,1)}, bf16[384,2048]{1,0:T(8,128)(2,1)}) custom-call(bf16[128,2048]{1,0:T(8,128)(2,1)} %x_ref.1, bf16[128,2048]{1,0:T(8,128)(2,1)} %g_ref.1, f32[16,128]{1,0:T(8,128)} %pad_maximum_fusion.meta_ref, ...), custom_call_target="tpu_custom_call" | custom-call | tf_op jit(solution)/shard_map/pallas_call | solution.py:549
  156.8 0.8 slice.3
  157.6 0.0 copy-done.2
  157.6 0.5 select_reduce_fusion
  158.2 1.9 %copy.16 = bf16[128,2048]{1,0:T(8,128)(2,1)} copy(bf16[128,2048]{1,0:T(8,128)(2,1)} %get-tuple-element.20) | data formatting | bytes 1048576
  160.1 0.0 copy-start.1
  160.1 2.8 %copy.17 = bf16[1,2048,384]{2,1,0:T(8,128)(2,1)} copy(bf16[1,2048,384]{2,1,0:T(8,128)(2,1)} %bitcast.16) | data formatting | bytes 3145728
  162.9 0.0 copy-done.1
  162.9 0.0 copy-start
  162.9 1.1 copy.18
  164.0 0.8 copy-done
  164.9 1.1 copy.19
  (1 shorter events, 0.0 us)
Async XLA Ops:
  3.4 154.2 %copy-start.2 = (s32[128,2]{0,1:T(2,128)S(1)}, s32[128,2]{0,1:T(2,128)}, u32[]{:S(2)}) copy-start(s32[128,2]{0,1:T(2,128)} %param.10) | copy-start | bytes 3076
  160.1 2.8 %copy-start.1 = (bf16[2048,384]{1,0:T(8,128)(2,1)S(1)}, bf16[2048,384]{1,0:T(8,128)(2,1)}, u32[]{:S(2)}) copy-start(bf16[2048,384]{1,0:T(8,128)(2,1)} %get-tuple-element.13) | copy-start | bytes 4718596
  162.9 2.0 %copy-start = (bf16[384,2048]{1,0:T(8,128)(2,1)S(1)}, bf16[384,2048]{1,0:T(8,128)(2,1)}, u32[]{:S(2)}) copy-start(bf16[384,2048]{1,0:T(8,128)(2,1)} %get-tuple-element.14) | copy-start | bytes 4718596
